TPU v7x, 512 devices: a whole 4x8x8 slice. The times are simulated.
512 devices in a mesh: strip: 8 (over x, core), dom: 64 (over y, z).
Axes of the slice: x: 4, y: 8, z: 8, core: 2. Of those that a mesh axis runs over, the one named last changes fastest.
Arguments:
- columns: bfloat16 [8, 196608, 128], P('strip', 'dom'), may hold values from -12 to 12
- regrid_weights: bfloat16 [8, 3072, 64, 128], P('strip', 'dom'), may hold values from 0.0019989014 to 0.059814453
- owner_table: int32 [8, 3072, 1], P('strip', 'dom'), may hold values from 0 to 63; in each aligned block of 48 rows (0 to 47, 48 to 95, ..., all dimensions but the last counted through in order) at most 2 rows name the same one
- grid_targets: int32 [8, 3072, 2], P('strip', 'dom'), may hold values from 0 to 15, all different within a row
- halo_send: int32 [8, 64, 2, 128], P('strip', 'dom'), may hold values from 0 to 3071
- halo_recv: int32 [8, 64, 2, 128], P('strip', 'dom'), may hold values from 0 to 3071
- coag: bfloat16 [128, 128], replicated, may hold values from -0.5 to 0.5
- settle_gain: float32 [128], replicated, may hold values from 2 to 20
Outputs:
- grid: bfloat16 [8, 65536, 128], P('strip', 'dom')
- columns_out: bfloat16 [8, 196608, 128], P('strip', 'dom')
Inputs may be any that keep to these rules, and one draw needn't show every extreme that they name: `owner_table`: among the 48 column blocks of one partition at most 2 have the same owner, and some partition has exactly 2 with one owner. `grid_targets`: the two grid blocks of a column block differ.
All inputs are finite; a program needn't handle non-finite values.
Results may differ from a plain program's by a relative error of at most 0.0045.
Values may be sent and summed in bfloat16 or wider, within the bound.
A program may use at most 64 MiB of HBM per device.

v0:
```python
import jax
import jax.numpy as jnp
from jax import lax
from jax.sharding import PartitionSpec as P

GB = 16


def from_behind(shard, axis, by):
    peers = lax.axis_size(axis)
    pairs = [(i, i + by) for i in range(peers) if 0 <= i + by < peers]
    return lax.ppermute(shard, axis, pairs)


def shards(
    columns, regrid_weights, owner_table, grid_targets, halo_send, halo_recv, coag, settle_gain
):
    partitions = lax.axis_size("dom")
    strip_count = lax.axis_size("strip")
    nblocks = regrid_weights.shape[1]
    block_cols = regrid_weights.shape[2]
    capacity = max(2, 2 * nblocks // partitions)
    slot_count = partitions * capacity
    local = columns[0]
    chans = local.shape[1]
    send_lists = halo_send[0, 0]
    recv_lists = halo_recv[0, 0]
    upper_rows = jnp.take(local, send_lists[0], axis=0)
    lower_rows = jnp.take(local, send_lists[1], axis=0)
    from_lower = from_behind(upper_rows, "strip", 1)
    from_upper = from_behind(lower_rows, "strip", -1)
    strip_id = lax.axis_index("strip")
    local_float = local.astype(jnp.float32)
    delta_lower = jnp.where(
        strip_id > 0,
        from_lower.astype(jnp.float32) - jnp.take(local_float, recv_lists[0], axis=0),
        0.0,
    )
    delta_upper = jnp.where(
        strip_id < strip_count - 1,
        from_upper.astype(jnp.float32) - jnp.take(local_float, recv_lists[1], axis=0),
        0.0,
    )
    all_rows = jnp.concatenate([recv_lists[0], recv_lists[1]], axis=0)
    relaxed = local_float.at[all_rows].add(
        0.5 * jnp.concatenate([delta_lower, delta_upper], axis=0)
    )
    owners = owner_table[0, :, 0]
    same_owner = owners[:, None] == owners[None, :]
    block_ids = jnp.arange(nblocks, dtype=jnp.int32)
    earlier = block_ids[None, :] < block_ids[:, None]
    owner_rank = jnp.sum((same_owner & earlier).astype(jnp.int32), axis=1)
    slot_index = owners * capacity + owner_rank
    col_blocks = local.reshape(nblocks, block_cols, chans)
    send_blocks = (
        jnp.zeros((slot_count, block_cols, chans), jnp.bfloat16).at[slot_index].set(col_blocks)
    )
    send_weights = (
        jnp.zeros((slot_count, block_cols, 2 * block_cols), jnp.bfloat16)
        .at[slot_index]
        .set(regrid_weights[0])
    )
    send_targets = (
        jnp.full((slot_count, 2), -1.0, jnp.bfloat16)
        .at[slot_index]
        .set(grid_targets[0].astype(jnp.bfloat16))
    )
    got_blocks, got_weights, got_targets = (
        lax.all_to_all(send_blocks, "dom", split_axis=0, concat_axis=0, tiled=True),
        lax.all_to_all(send_weights, "dom", split_axis=0, concat_axis=0, tiled=True),
        lax.all_to_all(send_targets, "dom", split_axis=0, concat_axis=0, tiled=True),
    )
    contrib = jnp.einsum(
        "rcq,rch->rqh", got_weights, got_blocks, preferred_element_type=jnp.float32
    )
    contrib = contrib.reshape(slot_count, 2, block_cols, chans)
    tile_ids = jnp.arange(GB, dtype=jnp.int32).astype(jnp.bfloat16)
    selector = got_targets[:, :, None] == tile_ids[None, None, :]
    selector_float = selector.astype(jnp.float32)
    numer = jnp.einsum("rkb,rkgh->bgh", selector_float, contrib, precision=lax.Precision.HIGHEST)
    col_total = jnp.sum(got_weights.astype(jnp.float32), axis=1).reshape(slot_count, 2, block_cols)
    denom = jnp.einsum("rkb,rkg->bg", selector_float, col_total, precision=lax.Precision.HIGHEST)
    grid = (numer / jnp.maximum(denom, 1.0)[:, :, None]).astype(jnp.bfloat16)
    mixed = jnp.dot(grid.reshape(-1, chans), coag, preferred_element_type=jnp.float32)
    flux = (
        (settle_gain[None, :] * jnp.tanh(mixed)).astype(jnp.bfloat16).reshape(GB, block_cols, chans)
    )
    picked = jnp.einsum(
        "rkb,bgh->rkgh", selector.astype(jnp.bfloat16), flux, preferred_element_type=jnp.float32
    )
    picked = picked.astype(jnp.bfloat16).reshape(slot_count, 2 * block_cols, chans)
    picked_home = lax.all_to_all(picked, "dom", split_axis=0, concat_axis=0, tiled=True)
    back_home = jnp.einsum(
        "rcq,rqh->rch", send_weights, picked_home, preferred_element_type=jnp.float32
    ).astype(jnp.bfloat16)
    returned = jnp.take(back_home, slot_index, axis=0).reshape(nblocks * block_cols, chans)
    columns_out = (relaxed + returned.astype(jnp.float32)).astype(jnp.bfloat16)
    return (grid.reshape(1, GB * block_cols, chans), columns_out[None])


def solution(mesh):
    placed = (
        P("strip", "dom", None),
        P("strip", "dom", None, None),
        P("strip", "dom", None),
        P("strip", "dom", None),
        P("strip", "dom", None, None),
        P("strip", "dom", None, None),
        P(),
        P(),
    )
    return jax.shard_map(
        shards,
        mesh=mesh,
        in_specs=placed,
        out_specs=(P("strip", "dom", None), P("strip", "dom", None)),
        check_vma=False,
    )
```

profile of v0, /device:TPU:40, one launch (start us, length us, event | category | flops | bytes accessed | tf_op | source)
XLA Modules:
  0.0 328.1 jit_solution(7579897978133364505)
XLA Ops:
  0.6 0.0 copy-start
  0.6 0.0 copy-start.3
  0.7 0.9 convert_reduce_fusion.1
  1.6 0.7 fusion.32
  2.2 0.7 convert_bitcast_fusion.1
  2.9 0.1 copy.44
  3.0 0.7 scatter_custom_fusion
  3.8 1.1 copy.46
  4.9 16.3 %all-to-all-start = ((bf16[64,2,2]{1,2,0:T(2,128)(2,1)}), bf16[64,2,2]{1,2,0:T(2,128)(2,1)S(1)}, u32[]{:S(2)}, u32[]{:S(2)}) async-start(bf16[64,2,2]{1,2,0:T(2,128)(2,1)} %copy.46), calls=%async_computation | async-start | bytes 65536 | tf_op jit(solution)/shard_map/all_to_all | solution.py:71
  21.2 1.9 broadcast.75.clone
  23.0 0.0 copy-done.3
  23.1 6.2 %scatter_fusion = bf16[128,64,128]{2,1,0:T(8,128)(2,1)} fusion(bf16[128,64,128]{2,1,0:T(8,128)(2,1)} %broadcast.75.clone, s32[48]{0:T(128)S(1)} %fusion.32, bf16[48,64,128]{2,1,0:T(8,128)(2,1)S(1)} %bitcast.85), kind=kCustom, calls=%fused_computation.6 | custom fusion | bytes 2359488 | tf_op jit(solution)/shard_map/scatter | solution.py:61
  29.3 0.0 all-to-all-done
  29.3 12.7 %all-to-all-start.1 = ((bf16[128,64,128]{2,1,0:T(8,128)(2,1)}), bf16[128,64,128]{2,1,0:T(8,128)(2,1)S(1)}, u32[]{:S(2)}, u32[]{:S(2)}) async-start(bf16[128,64,128]{2,1,0:T(8,128)(2,1)} %scatter_fusion), calls=%async_computation.1 | async-start | bytes 4194304 | tf_op jit(solution)/shard_map/all_to_all | solution.py:70
  42.0 0.0 copy-start.1
  42.0 1.8 broadcast.75.clone.1
  43.9 0.0 copy-done.1
  43.9 6.3 %scatter_fusion.1 = bf16[128,64,128]{2,1,0:T(8,128)(2,1)} fusion(bf16[128,64,128]{2,1,0:T(8,128)(2,1)} %broadcast.75.clone.1, s32[48]{0:T(128)S(1)} %fusion.32, bf16[48,64,128]{2,1,0:T(8,128)(2,1)S(1)} %bitcast.79), kind=kCustom, calls=%fused_computation.7 | custom fusion | bytes 2359488 | tf_op jit(solution)/shard_map/scatter | solution.py:56
  50.1 44.6 %all-to-all-done.1 = bf16[128,64,128]{2,1,0:T(8,128)(2,1)S(1)} async-done(((bf16[128,64,128]{2,1,0:T(8,128)(2,1)}), bf16[128,64,128]{2,1,0:T(8,128)(2,1)S(1)}, u32[]{:S(2)}, u32[]{:S(2)}) %all-to-all-start.1) | async-done | bytes 2097184 | tf_op jit(solution)/shard_map/all_to_all | solution.py:70
  94.7 10.6 %all-to-all-start.2 = ((bf16[128,64,128]{2,1,0:T(8,128)(2,1)}), bf16[128,64,128]{2,1,0:T(8,128)(2,1)}, u32[]{:S(2)}, u32[]{:S(2)}) async-start(bf16[128,64,128]{2,1,0:T(8,128)(2,1)} %scatter_fusion.1), calls=%async_computation.2 | async-start | bytes 4194304 | tf_op jit(solution)/shard_map/all_to_all | solution.py:69
  105.3 0.1 eq.34
  105.5 0.7 convert_reduce_fusion
  106.2 0.1 copy.49
  106.3 0.2 fusion.13
  106.4 0.1 copy.50
  106.5 49.5 %all-to-all-done.2 = bf16[128,64,128]{2,1,0:T(8,128)(2,1)} async-done(((bf16[128,64,128]{2,1,0:T(8,128)(2,1)}), bf16[128,64,128]{2,1,0:T(8,128)(2,1)}, u32[]{:S(2)}, u32[]{:S(2)}) %all-to-all-start.2) | async-done | bytes 2097184 | tf_op jit(solution)/shard_map/all_to_all | solution.py:69
  156.0 2.9 fusion.33
  159.0 0.0 copy-start.6
  159.0 7.7 %fusion.9 = bf16[16,64,128]{2,0,1:T(8,128)(2,1)S(1)} fusion(f32[128,2,64,128]{3,2,1,0:T(8,128)S(1)} %bitcast.77, f32[16,64]{0,1:T(8,128)S(1)} %copy.50, bf16[128,2]{0,1:T(2,128)(2,1)S(1)} %eq.34, bf16[16]{0:T(256)(128)(2,1)S(1)} %iota_convert_fusion), kind=kOutput, calls=%fused_computation.19 | convolution fusion | flops 402927616 | bytes 8655392 | tf_op jit(solution)/shard_map/rkb,rkgh->bgh/dot_general | solution.py:80
  166.7 0.1 copy.51
  166.7 0.0 copy-start.2
  166.8 0.0 copy-done
  166.8 0.0 copy-done.6
  166.8 0.2 fusion.12
  167.0 1.4 convolution_convert_fusion
  168.4 0.0 copy-done.2
  168.4 4.9 %copy.54 = bf16[128,128,128]{2,1,0:T(8,128)(2,1)} copy(bf16[128,128,128]{2,0,1:T(8,128)(2,1)S(1)} %bitcast.78) | data formatting | bytes 8388608 | tf_op jit(solution)/shard_map/reshape | solution.py:91
  173.3 0.0 copy-start.5
  173.3 0.0 copy-start.4
  173.3 9.5 %all-to-all-start.3 = ((bf16[128,128,128]{2,1,0:T(8,128)(2,1)}), bf16[128,128,128]{2,1,0:T(8,128)(2,1)}, u32[]{:S(2)}, u32[]{:S(2)}) async-start(bf16[128,128,128]{2,1,0:T(8,128)(2,1)} %copy.54), calls=%async_computation.3 | async-start | bytes 8388608 | tf_op jit(solution)/shard_map/all_to_all | solution.py:92
  182.8 0.0 copy-done.5
  182.8 0.7 gather_fusion.3
  183.5 0.1 broadcast_select_fusion
  183.6 1.3 collective-permute-start.1
  185.0 0.7 gather_fusion.1
  185.7 0.1 broadcast_select_fusion.1
  185.8 3.0 collective-permute-start
  188.8 0.0 copy-done.4
  188.9 0.0 copy-done.7
  188.9 0.1 bitcast_convert_fusion
  189.0 0.1 broadcast_in_dim.54
  189.1 0.1 broadcast_in_dim.55
  189.2 0.6 gather_fusion.4
  189.8 0.6 gather_fusion.2
  190.5 0.0 collective-permute-done.1
  190.5 0.1 fusion.19
  190.6 0.0 collective-permute-done
  190.6 0.1 fusion.20
  190.7 125.7 %all-to-all-done.3 = bf16[128,128,128]{2,1,0:T(8,128)(2,1)} async-done(((bf16[128,128,128]{2,1,0:T(8,128)(2,1)}), bf16[128,128,128]{2,1,0:T(8,128)(2,1)}, u32[]{:S(2)}, u32[]{:S(2)}) %all-to-all-start.3) | async-done | bytes 4194336 | tf_op jit(solution)/shard_map/all_to_all | solution.py:92
  316.4 4.0 %convolution_convert_fusion.1 = bf16[128,64,128]{2,1,0:T(8,128)(2,1)S(1)} fusion(bf16[128,64,128]{2,1,0:T(8,128)(2,1)} %scatter_fusion, bf16[128,128,128]{2,1,0:T(8,128)(2,1)} %all-to-all-done.3), kind=kOutput, calls=%fused_computation.13 | convolution fusion | flops 269484032 | bytes 8388608 | tf_op jit(solution)/shard_map/rcq,rqh->rch/dot_general | solution.py:93
  320.5 1.6 gather_fusion
  322.0 2.6 convert_add_fusion
  324.6 2.5 scatter_custom_fusion.3
  327.1 1.0 convert_bitcast_fusion
  (13 shorter events, 0.1 us)
Async XLA Ops:
  0.6 166.1 %copy-start = (bf16[128,128]{1,0:T(8,128)(2,1)S(1)}, bf16[128,128]{1,0:T(8,128)(2,1)}, u32[]{:S(2)}) copy-start(bf16[128,128]{1,0:T(8,128)(2,1)} %param.18) | copy-start | bytes 98308
  0.6 22.4 %copy-start.3 = (bf16[1,48,64,128]{3,2,1,0:T(8,128)(2,1)S(1)}, bf16[1,48,64,128]{3,2,1,0:T(8,128)(2,1)}, u32[]{:S(2)}) copy-start(bf16[1,48,64,128]{3,2,1,0:T(8,128)(2,1)} %param.13) | copy-start | bytes 2359300
  4.9 24.4 %all-to-all-start = ((bf16[64,2,2]{1,2,0:T(2,128)(2,1)}), bf16[64,2,2]{1,2,0:T(2,128)(2,1)S(1)}, u32[]{:S(2)}, u32[]{:S(2)}) async-start(bf16[64,2,2]{1,2,0:T(2,128)(2,1)} %copy.46), calls=%async_computation | async-start | bytes 65536 | tf_op jit(solution)/shard_map/all_to_all | solution.py:71
  29.3 65.4 %all-to-all-start.1 = ((bf16[128,64,128]{2,1,0:T(8,128)(2,1)}), bf16[128,64,128]{2,1,0:T(8,128)(2,1)S(1)}, u32[]{:S(2)}, u32[]{:S(2)}) async-start(bf16[128,64,128]{2,1,0:T(8,128)(2,1)} %scatter_fusion), calls=%async_computation.1 | async-start | bytes 4194304 | tf_op jit(solution)/shard_map/all_to_all | solution.py:70
  42.0 1.9 copy-start.1
  94.7 61.3 %all-to-all-start.2 = ((bf16[128,64,128]{2,1,0:T(8,128)(2,1)}), bf16[128,64,128]{2,1,0:T(8,128)(2,1)}, u32[]{:S(2)}, u32[]{:S(2)}) async-start(bf16[128,64,128]{2,1,0:T(8,128)(2,1)} %scatter_fusion.1), calls=%async_computation.2 | async-start | bytes 4194304 | tf_op jit(solution)/shard_map/all_to_all | solution.py:69
  159.0 7.8 %copy-start.6 = (f32[128]{0:T(128)S(1)}, f32[128]{0:T(128)}, u32[]{:S(2)}) copy-start(f32[128]{0:T(128)} %param.19) | copy-start | bytes 1540
  166.7 1.6 copy-start.2
  173.3 9.5 %copy-start.5 = (s32[1,1,2,128]{3,2,1,0:T(2,128)S(1)}, s32[1,1,2,128]{3,2,1,0:T(2,128)}, u32[]{:S(2)}) copy-start(s32[1,1,2,128]{3,2,1,0:T(2,128)} %param.16) | copy-start | bytes 3076
  173.3 15.5 %copy-start.4 = (s32[1,1,2,128]{3,2,1,0:T(2,128)S(1)}, s32[1,1,2,128]{3,2,1,0:T(2,128)}, u32[]{:S(2)}) copy-start(s32[1,1,2,128]{3,2,1,0:T(2,128)} %param.17) | copy-start | bytes 3076
  173.3 15.6 %copy-start.7 = (s32[1,48,1]{1,2,0:T(1,128)S(1)}, s32[1,48,1]{1,2,0:T(1,128)}, u32[]{:S(2)}) copy-start(s32[1,48,1]{1,2,0:T(1,128)} %param.14) | copy-start | bytes 580
  173.3 143.1 %all-to-all-start.3 = ((bf16[128,128,128]{2,1,0:T(8,128)(2,1)}), bf16[128,128,128]{2,1,0:T(8,128)(2,1)}, u32[]{:S(2)}, u32[]{:S(2)}) async-start(bf16[128,128,128]{2,1,0:T(8,128)(2,1)} %copy.54), calls=%async_computation.3 | async-start | bytes 8388608 | tf_op jit(solution)/shard_map/all_to_all | solution.py:92
  183.6 6.9 %collective-permute-start.1 = (bf16[128,128]{1,0:T(8,128)(2,1)S(1)}, bf16[128,128]{1,0:T(8,128)(2,1)S(1)}, u32[]{:S(2)}, u32[]{:S(2)}) collective-permute-start(bf16[128,128]{1,0:T(8,128)(2,1)S(1)} %broadcast_select_fusion), channel_id=1, source_target_pairs={{64,0},{128,64},{192,128},{256,192},{320,256},{384,320},{448,384},... | collective-permute-start | bytes 98312 | tf_op jit(solution)/shard_map/ppermute | solution.py:12
  185.8 4.8 %collective-permute-start = (bf16[128,128]{1,0:T(8,128)(2,1)S(1)}, bf16[128,128]{1,0:T(8,128)(2,1)S(1)}, u32[]{:S(2)}, u32[]{:S(2)}) collective-permute-start(bf16[128,128]{1,0:T(8,128)(2,1)S(1)} %broadcast_select_fusion.1), channel_id=1, source_target_pairs={{0,64},{64,128},{128,192},{192,256},{256,320},{320,384},{384,448},... | collective-permute-start | bytes 98312 | tf_op jit(solution)/shard_map/ppermute | solution.py:12
where the time goes:
time: 329 us; the launch traced here: 328 us
  waiting for transfers between devices  220 us (67%)
  starting transfers between devices  53.4 us (16%)
  local copies, waits for them, and re-layouts  27.9 us (8%)
  matrix products  16.4 us (5%)
  other arithmetic  9.5 us (3%)
    all_to_all x1, waiting for transfers between devices, shards(): lax.all_to_all(picked, 'dom', split_axis=0, concat_axis=0, tiled=True)  126 us
    all_to_all x1, waiting for transfers between devices, shards(): lax.all_to_all(send_blocks, 'dom', split_axis=0, concat_axis=0, tiled=True)  49.5 us
    all_to_all x1, waiting for transfers between devices, shards(): lax.all_to_all(send_weights, 'dom', split_axis=0, concat_axis=0, tiled=True)  44.6 us
    all_to_all x1, starting transfers between devices, shards(): lax.all_to_all(send_targets, 'dom', split_axis=0, concat_axis=0, tiled=True)  16.3 us
    all_to_all x1, starting transfers between devices, shards(): lax.all_to_all(send_weights, 'dom', split_axis=0, concat_axis=0, tiled=True)  12.7 us
    all_to_all x1, starting transfers between devices, shards(): lax.all_to_all(send_blocks, 'dom', split_axis=0, concat_axis=0, tiled=True)  10.6 us
    all_to_all x1, starting transfers between devices, shards(): lax.all_to_all(picked, 'dom', split_axis=0, concat_axis=0, tiled=True)  9.5 us
    dot_general x1, matrix products, shards(): jnp.einsum('rkb,rkgh->bgh', selector_float, contrib, precision=lax.Precis...  7.7 us
  transfers between devices with their start and end apart: 6, of which 3 were waited for; matrix products, arithmetic and copies ran while one was open for 6% of the time, Pallas kernels for 0%

commit v1 on v0

v1 whole, which is shorter than its diff:
```python
import functools
import jax
import jax.numpy as jnp
from jax import lax
from jax.experimental import pallas as pl
from jax.experimental.pallas import tpu as pltpu
from jax.sharding import PartitionSpec as P

MESH = pl.DeviceIdType.MESH
BF = jnp.bfloat16
F32 = jnp.float32
SIDE = 8
ORDER = (4, 3, 5, 2, 6, 1, 7)
PAIRS = ((0, 4), (3, 5), (2, 6), (1, 7))
CHUNK = 1040


def kernel(
    tab, slot_of, tsel, cols, wts, hsend_idx, hrecv_idx, coag, gain,
    grid_out, cols_out,
    abuf_s, abuf_r, tf, tr, wexp, acc, den, bsend, brecv, dtot, flux, dsend, drecv,
    relaxed, hrows, hsend, hrecv,
    a_s, a_r, b_s, b_r, c_s, c_r, d_s, d_r, h_s, h_r,
):
    strip = lax.axis_index("strip")
    dom = lax.axis_index("dom")
    strips = lax.axis_size("strip")
    y = dom // SIDE
    z = lax.rem(dom, SIDE)
    q = lax.rem(y + z, 2)

    def along(cls, dist):
        ny = lax.rem(y + (1 - cls) * dist + SIDE, SIDE)
        nz = lax.rem(z + cls * dist + SIDE, SIDE)
        return (strip, ny * SIDE + nz)

    barrier = pltpu.get_barrier_semaphore()
    for cls in range(2):
        for dist in range(1, SIDE):
            pl.semaphore_signal(barrier, inc=1, device_id=along(cls, dist), device_id_type=MESH)

    @pl.when(strip > 0)
    def _():
        pl.semaphore_signal(barrier, inc=1, device_id=(strip - 1, dom), device_id_type=MESH)

    @pl.when(strip < strips - 1)
    def _():
        pl.semaphore_signal(barrier, inc=1, device_id=(strip + 1, dom), device_id_type=MESH)

    def pack(dst, cls, dist):
        base = cls * 64 + dist * 8

        def one(s, carry):
            j = tab[base + s]
            dst[pl.ds(pl.multiple_of(s * 64, 64), 64), :] = cols[j]
            dst[pl.ds(pl.multiple_of(512 + s * 64, 64), 64), :] = wts[j]
            return carry

        lax.fori_loop(0, 8, one, 0)
        dst[pl.ds(1024, 16), :] = tsel[cls * 8 + dist]

    def pack_far(t, carry):
        cls, dist = t // 7, lax.rem(t, 7) + 1
        pack(abuf_s.at[cls, dist - 1], cls, dist)
        return carry

    lax.fori_loop(0, 14, pack_far, 0)

    neighbours = (strip > 0).astype(jnp.int32) + (strip < strips - 1).astype(jnp.int32)
    pl.semaphore_wait(barrier, 14 + neighbours)

    def a_copy(cls, dist):
        return pltpu.make_async_remote_copy(
            abuf_s.at[cls, dist - 1], abuf_r.at[cls, dist],
            a_s.at[cls, dist - 1], a_r.at[cls, dist - 1],
            device_id=along(cls, dist), device_id_type=MESH,
        )

    for dist in ORDER:
        for cls in range(2):
            a_copy(cls, dist).start()

    for cls in range(2):
        pack(abuf_r.at[cls, 0], cls, 0)

    idx = jnp.concatenate(
        [hsend_idx[...], hrecv_idx[...], jnp.zeros((4, 128), jnp.int32)], axis=0
    ).astype(F32)
    idx_t = idx.T
    hrows[...] = jnp.zeros_like(hrows)

    def gather(kc, carry):
        block = cols[pl.ds(kc * 4, 4)].reshape(256, 128)
        lane = lax.broadcasted_iota(jnp.int32, (128, 256), 1) + kc * 256
        lane = lane.astype(F32)
        for l in range(4):
            hot = jnp.where(idx_t[:, l : l + 1] == lane, 1.0, 0.0).astype(BF)
            hrows[l] += jnp.dot(hot, block, preferred_element_type=F32)
        return carry

    lax.fori_loop(0, 12, gather, 0)
    hsend[...] = hrows[pl.ds(0, 2)].astype(BF)

    def h_copy(way):
        step = 1 - 2 * way
        return pltpu.make_async_remote_copy(
            hsend.at[way], hrecv.at[way], h_s.at[way], h_r.at[way],
            device_id=(strip + step, dom), device_id_type=MESH,
        )

    @pl.when(strip < strips - 1)
    def _():
        h_copy(0).start()

    @pl.when(strip > 0)
    def _():
        h_copy(1).start()

    par = jnp.where(lax.broadcasted_iota(jnp.int32, (1, 128), 1) >= 64, 1.0, 0.0)
    twice = 2.0 * lax.broadcasted_iota(jnp.int32, (8, 128), 0).astype(F32)
    den[...] = jnp.zeros_like(den)

    def expand(cls, i, o, d, row0):
        for rr in range(2):
            w = abuf_r[cls, d, pl.ds(pl.multiple_of(512 + i * 128 + rr * 64, 64), 64), :]
            u = tf[cls, d, pl.ds(2 * i + rr, 1), :] - par
            v = tr[cls, d, pl.ds(2 * i + rr, 1), :] - par
            wf = w.astype(F32)
            wrf = pltpu.roll(wf, 64, 1)
            wr = wrf.astype(BF)
            total = jnp.sum(wf, axis=0, keepdims=True)
            turned = jnp.sum(wrf, axis=0, keepdims=True)
            den[o] += jnp.where(u == twice, total, 0.0) + jnp.where(v == twice, turned, 0.0)
            ub = jnp.broadcast_to(u, (16, 128))
            vb = jnp.broadcast_to(v, (16, 128))
            for m in range(8):
                a = jnp.where(ub == 2.0 * m, 1.0, 0.0).astype(BF)
                b = jnp.where(vb == 2.0 * m, 1.0, 0.0).astype(BF)
                a4 = jnp.concatenate([a] * 4, axis=0)
                b4 = jnp.concatenate([b] * 4, axis=0)
                wexp[o, pl.ds(row0 + rr * 64, 64), pl.ds(m * 128, 128)] = w * a4 + wr * b4

    def tile_step(pos, cls, i):
        o = cls * 4 + i
        d1, d2 = PAIRS[pos]
        expand(cls, i, o, d1, pos * 256)
        expand(cls, i, o, d2, pos * 256 + 128)
        rows = pl.ds(pl.multiple_of(i * 128, 128), 128)
        xt = jnp.concatenate([abuf_r[cls, d1, rows, :].T, abuf_r[cls, d2, rows, :].T], axis=1)
        for mm in range(4):
            lanes = pl.ds(mm * 256, 256)
            part = jnp.dot(
                xt, wexp[o, pl.ds(pos * 256, 256), lanes], preferred_element_type=F32
            )
            if pos == 0:
                acc[o, :, lanes] = part
            else:
                acc[o, :, lanes] += part

    def arrive(pos, cls):
        for d in PAIRS[pos]:
            if d > 0:
                a_copy(cls, d).wait_recv()
            t = abuf_r[cls, d, pl.ds(1024, 16), :].astype(F32)[0:8]
            tf[cls, d] = t
            tr[cls, d] = pltpu.roll(t, 64, 1)

    for pos in range(3):

        def half(cls, carry, pos=pos):
            arrive(pos, cls)

            def tile(i, c):
                tile_step(pos, cls, i)
                return c

            return lax.fori_loop(0, 4, tile, carry)

        lax.fori_loop(0, 2, half, 0)

    @pl.when(strip > 0)
    def _():
        h_copy(0).wait_recv()

    @pl.when(strip == 0)
    def _():
        hrecv[0] = jnp.zeros((128, 128), BF)

    @pl.when(strip < strips - 1)
    def _():
        h_copy(1).wait_recv()

    @pl.when(strip == strips - 1)
    def _():
        hrecv[1] = jnp.zeros((128, 128), BF)

    keep = (
        jnp.where(strip > 0, 0.5, 0.0).astype(F32),
        jnp.where(strip < strips - 1, 0.5, 0.0).astype(F32),
    )
    for way in range(2):
        delta = keep[way] * (hrecv[way].astype(F32) - hrows[2 + way])
        high = delta.astype(BF)
        hrows[2 + way] = delta
        hsplit = (high, (delta - high.astype(F32)).astype(BF))
        if way == 0:
            split0 = hsplit
        else:
            split1 = hsplit
    highs = jnp.concatenate([split0[0], split1[0]], axis=0)
    lows = jnp.concatenate([split0[1], split1[1]], axis=0)

    def relax(kc, carry):
        row = (lax.broadcasted_iota(jnp.int32, (256, 128), 0) + kc * 256)
        hot = jnp.concatenate(
            [
                jnp.where(row == hrecv_idx[pl.ds(0, 1), :], 1.0, 0.0).astype(BF),
                jnp.where(row == hrecv_idx[pl.ds(1, 1), :], 1.0, 0.0).astype(BF),
            ],
            axis=1,
        )
        moved = jnp.dot(hot, highs, preferred_element_type=F32)
        moved += jnp.dot(hot, lows, preferred_element_type=F32)
        block = cols[pl.ds(kc * 4, 4)].reshape(256, 128).astype(F32)
        relaxed[pl.ds(kc * 4, 4)] = (block + moved).reshape(4, 64, 128)
        return carry

    lax.fori_loop(0, 12, relax, 0)

    def b_parts(cls, a):
        dist = 2 * a + (1 - cls) * q + cls * (1 - q)
        coord = (1 - cls) * z + cls * y
        i = lax.rem(coord + dist, SIDE) // 2
        return dist, i

    def b_copy(cls, a):
        dist, i = b_parts(cls, a)
        slot = jnp.maximum(dist, 1) - 1
        return pltpu.make_async_remote_copy(
            bsend.at[cls * 4 + i], brecv.at[slot], b_s.at[cls, a], b_r.at[slot],
            device_id=along(1 - cls, dist), device_id_type=MESH,
        )

    for cls in range(2):
        arrive(3, cls)

    def last(t, carry):
        cls, a = lax.rem(t, 2), t // 2
        dist, i = b_parts(cls, a)
        tile_step(3, cls, i)
        o = cls * 4 + i

        @pl.when(dist > 0)
        def _():
            for m in range(8):
                bsend[o, pl.ds(m * 128, 128), :] = acc[o, :, pl.ds(m * 128, 128)].astype(BF)
            dd = den[o]
            high = dd.astype(BF)
            low = (dd - high.astype(F32)).astype(BF)
            bsend[o, pl.ds(1024, 16), :] = jnp.concatenate([high, low], axis=0)
            b_copy(cls, a).start()

        return carry

    lax.fori_loop(0, 8, last, 0)

    own = q * 4 + ((1 - q) * z + q * y) // 2
    dsum = den[own]
    for d in range(7):
        pltpu.make_async_remote_copy(
            bsend.at[0], brecv.at[d], b_s.at[0, 0], b_r.at[d],
            device_id=along(0, 1), device_id_type=MESH,
        ).wait_recv()
        two = brecv[d, pl.ds(1024, 16), :].astype(F32)
        dsum = dsum + two[0:8] + two[8:16]
    dtot[...] = jnp.maximum(dsum, 1.0)

    def finish(m, carry):
        rows = pl.ds(pl.multiple_of(m * 128, 128), 128)
        num = acc[own, :, rows]
        for d in range(7):
            num += brecv[d, rows, :].astype(F32)
        g = (num / dtot[pl.ds(m, 1), :]).T.astype(BF)
        grid_out[rows, :] = g
        mixed = jnp.dot(g, coag[...], preferred_element_type=F32)
        flux[own, rows, :] = (gain[...] * jnp.tanh(mixed)).astype(BF)
        return carry

    lax.fori_loop(0, 8, finish, 0)

    def c_copy(dist):
        return pltpu.make_async_remote_copy(
            flux.at[own], flux.at[own], c_s.at[dist - 1], c_r.at[own],
            device_id=along(1 - q, dist), device_id_type=MESH,
        )

    for dist in ORDER:
        c_copy(dist).start()

    def d_copy(cls, i, dist):
        pair = pl.ds(i * 2, 2)
        o = cls * 4 + i
        return pltpu.make_async_remote_copy(
            dsend.at[cls, dist - 1, pair], drecv.at[pl.ds(cls * 64 + dist * 8 + i * 2, 2)],
            d_s.at[o, dist - 1], d_r.at[o, dist - 1],
            device_id=along(cls, SIDE - dist), device_id_type=MESH,
        )

    def back(t, carry):
        o = lax.rem(own + t, 8)
        cls, i = o // 4, lax.rem(o, 4)

        @pl.when(t > 0)
        def _():
            pltpu.make_async_remote_copy(
                flux.at[o], flux.at[o], c_s.at[0], c_r.at[o],
                device_id=along(0, 1), device_id_type=MESH,
            ).wait_recv()

        tile = flux[o]
        for pos in range(4):
            r = jnp.dot(
                wexp[o, pl.ds(pos * 256, 256), :], tile, preferred_element_type=F32
            ).astype(BF)
            for h in range(2):
                d = PAIRS[pos][h]
                two = r[h * 128 : h * 128 + 128].reshape(2, 64, 128)
                if d == 0:
                    drecv[pl.ds(cls * 64 + i * 2, 2)] = two
                else:
                    dsend[cls, d - 1, pl.ds(i * 2, 2)] = two
        for dist in ORDER:
            d_copy(cls, i, dist).start()
        return carry

    lax.fori_loop(0, 8, back, 0)

    def gather_back(o, carry):
        for dist in range(1, SIDE):
            d_copy(o // 4, lax.rem(o, 4), dist).wait_recv()
        return carry

    lax.fori_loop(0, 8, gather_back, 0)

    def final(j, carry):
        cols_out[j] = (relaxed[j] + drecv[slot_of[j]].astype(F32)).astype(BF)
        return carry

    lax.fori_loop(0, 48, final, 0)

    for dist in range(1, SIDE):
        for cls in range(2):
            a_copy(cls, dist).wait_send()
        c_copy(dist).wait_send()

    @pl.when(strip < strips - 1)
    def _():
        h_copy(0).wait_send()

    @pl.when(strip > 0)
    def _():
        h_copy(1).wait_send()

    def b_sent(t, carry):
        cls, a = lax.rem(t, 2), t // 2

        @pl.when(b_parts(cls, a)[0] > 0)
        def _():
            b_copy(cls, a).wait_send()

        return carry

    lax.fori_loop(0, 8, b_sent, 0)

    def d_sent(o, carry):
        for dist in range(1, SIDE):
            d_copy(o // 4, lax.rem(o, 4), dist).wait_send()
        return carry

    lax.fori_loop(0, 8, d_sent, 0)


def shards(
    columns, regrid_weights, owner_table, grid_targets, halo_send, halo_recv, coag, settle_gain
):
    nblocks, blk, chans = regrid_weights.shape[1], regrid_weights.shape[2], columns.shape[2]
    dom = lax.axis_index("dom")
    y, z = dom // SIDE, lax.rem(dom, SIDE)
    owners = owner_table[0, :, 0]
    ids = jnp.arange(nblocks, dtype=jnp.int32)
    rank = jnp.sum(
        ((owners[:, None] == owners[None, :]) & (ids[None, :] < ids[:, None])).astype(jnp.int32),
        axis=1,
    )
    oy, oz = owners // SIDE, lax.rem(owners, SIDE)
    cls = lax.rem(oy + oz, 2)
    dist = jnp.where(cls == 0, oy - y + SIDE, oz - z + SIDE) % SIDE
    slot_of = cls * 64 + dist * 8 + jnp.where(cls == 0, oz, oy) // 2 * 2 + rank
    hot = slot_of[None, :] == jnp.arange(128, dtype=jnp.int32)[:, None]
    tab = jnp.max(jnp.where(hot, ids[None, :], 0), axis=1)
    t01 = jnp.max(jnp.where(hot[:, None, :], grid_targets[0].T[None], -1), axis=2)
    tsel = jnp.repeat(t01, 64, axis=1).astype(BF).reshape(16, 8, 128)
    tsel = jnp.concatenate([tsel, tsel], axis=1)

    vmem = pl.BlockSpec(memory_space=pltpu.VMEM)
    smem = pl.BlockSpec(memory_space=pltpu.SMEM)
    dma = pltpu.SemaphoreType.DMA
    grid, out = pl.pallas_call(
        kernel,
        out_shape=(
            jax.ShapeDtypeStruct((1024, chans), BF),
            jax.ShapeDtypeStruct((nblocks, blk, chans), BF),
        ),
        in_specs=[smem, smem] + [vmem] * 7,
        out_specs=(vmem, vmem),
        scratch_shapes=[
            pltpu.VMEM((2, 7, CHUNK, 128), BF),
            pltpu.VMEM((2, 8, CHUNK, 128), BF),
            pltpu.VMEM((2, 8, 8, 128), F32),
            pltpu.VMEM((2, 8, 8, 128), F32),
            pltpu.VMEM((8, 1024, 1024), BF),
            pltpu.VMEM((8, 128, 1024), F32),
            pltpu.VMEM((8, 8, 128), F32),
            pltpu.VMEM((8, CHUNK, 128), BF),
            pltpu.VMEM((7, CHUNK, 128), BF),
            pltpu.VMEM((8, 128), F32),
            pltpu.VMEM((8, 1024, 128), BF),
            pltpu.VMEM((2, 7, 8, 64, 128), BF),
            pltpu.VMEM((128, 64, 128), BF),
            pltpu.VMEM((48, 64, 128), F32),
            pltpu.VMEM((4, 128, 128), F32),
            pltpu.VMEM((2, 128, 128), BF),
            pltpu.VMEM((2, 128, 128), BF),
            dma((2, 7)), dma((2, 7)),
            dma((2, 4)), dma((7,)),
            dma((7,)), dma((8,)),
            dma((8, 7)), dma((8, 7)),
            dma((2,)), dma((2,)),
        ],
        compiler_params=pltpu.CompilerParams(
            collective_id=0, has_side_effects=True, vmem_limit_bytes=56 * 2**20
        ),
    )(
        tab, slot_of, tsel,
        columns[0].reshape(nblocks, blk, chans), regrid_weights[0],
        halo_send[0, 0], halo_recv[0, 0], coag, settle_gain[None, :],
    )
    return grid[None], out.reshape(1, nblocks * blk, chans)


def solution(mesh):
    placed = (
        P("strip", "dom", None),
        P("strip", "dom", None, None),
        P("strip", "dom", None),
        P("strip", "dom", None),
        P("strip", "dom", None, None),
        P("strip", "dom", None, None),
        P(),
        P(),
    )
    return jax.shard_map(
        shards,
        mesh=mesh,
        in_specs=placed,
        out_specs=(P("strip", "dom", None), P("strip", "dom", None)),
        check_vma=False,
    )
```

time: 329 us -> 172 us (0.52)
  the two profiles are of different devices: /device:TPU:40 before, /device:TPU:1 now
where the time goes in v1:
time: 172 us
  Pallas kernels  164 us (95%)
  local copies, waits for them, and re-layouts  5.42 us (3%)
    pallas_call x1, Pallas kernels, shards(): pl.pallas_call(kernel, out_shape=(jax.ShapeDtypeStruct((1024, chans), BF)...  164 us
    unnamed x8, local copies, waits for them, and re-layouts  4.99 us

profile of v1, /device:TPU:1, one launch (start us, length us, event | category | flops | bytes accessed | tf_op | source)
XLA Modules:
  0.0 171.9 jit_solution(13341614874084262132)
XLA Ops:
  0.6 0.0 copy-start.2
  0.7 0.6 copy-done.2
  1.3 0.2 convert_reduce_fusion
  1.5 0.0 copy-start
  1.5 0.6 select_reduce_fusion.1.tab
  2.1 0.0 copy-done
  2.1 0.0 copy-start.1
  2.1 0.1 iota_compare_fusion
  2.2 0.6 copy-done.1
  2.8 0.1 select_reduce_fusion
  2.9 0.1 copy.10
  3.0 0.2 broadcast_in_dim.53
  3.3 0.1 convert_element_type.13
  3.4 0.6 pad_maximum_fusion.tsel
  4.0 164.2 %shard_map.95 = (bf16[1024,128]{1,0:T(8,128)(2,1)}, bf16[48,64,128]{2,1,0:T(8,128)(2,1)}) custom-call(s32[128]{0:T(128)} %select_reduce_fusion.1.tab, s32[48]{0:T(128)} %copy-done, bf16[16,16,128]{2,1,0:T(8,128)(2,1)} %pad_maximum_fusion.tsel, bf16[48,64,128]{2,1,0:T(8,128)(2,1)} %bitcast.12, bf16[48,64,128]{2,1,0:T(8,128)(2,1)} %bitcast.13, ...), custom_call_target="tpu_custom_call" | custom-call | tf_op jit(solution)/shard_map/pallas_call | solution.py:408
  168.2 1.7 copy.13
  169.9 2.1 %copy.14 = bf16[1,3072,128]{2,1,0:T(8,128)(2,1)} copy(bf16[1,3072,128]{2,1,0:T(8,128)(2,1)} %bitcast.14) | data formatting | bytes 1572864
  (2 shorter events, 0.0 us)
Async XLA Ops:
  0.6 0.7 copy-start.2
  1.5 0.6 copy-start
  2.1 0.7 copy-start.1

commit v2 on v1

--- a/solution.py
+++ b/solution.py
@@ -148,14 +148,15 @@
         rows = pl.ds(pl.multiple_of(i * 128, 128), 128)
         xt = jnp.concatenate([abuf_r[cls, d1, rows, :].T, abuf_r[cls, d2, rows, :].T], axis=1)
         for mm in range(4):
-            lanes = pl.ds(mm * 256, 256)
             part = jnp.dot(
-                xt, wexp[o, pl.ds(pos * 256, 256), lanes], preferred_element_type=F32
+                xt, wexp[o, pl.ds(pos * 256, 256), pl.ds(mm * 256, 256)], preferred_element_type=F32
             )
-            if pos == 0:
-                acc[o, :, lanes] = part
-            else:
-                acc[o, :, lanes] += part
+            for h in range(2):
+                piece = part[:, h * 128 : h * 128 + 128]
+                if pos == 0:
+                    acc[o, 2 * mm + h] = piece
+                else:
+                    acc[o, 2 * mm + h] += piece
 
     def arrive(pos, cls):
         for d in PAIRS[pos]:
@@ -227,75 +228,107 @@
 
     lax.fori_loop(0, 12, relax, 0)
 
-    def b_parts(cls, a):
-        dist = 2 * a + (1 - cls) * q + cls * (1 - q)
-        coord = (1 - cls) * z + cls * y
-        i = lax.rem(coord + dist, SIDE) // 2
-        return dist, i
-
-    def b_copy(cls, a):
-        dist, i = b_parts(cls, a)
-        slot = jnp.maximum(dist, 1) - 1
+    hcoord = (1 - q) * z + q * y
+    ccoord = (1 - q) * y + q * z
+
+    def tile_at(home, t):
+        coord = hcoord if home else ccoord
+        return (q if home else 1 - q) * 4 + lax.rem(coord + t + SIDE, SIDE) // 2
+
+    def next_to(home, way):
+        return along(1 - q if home else q, 1 - 2 * way)
+
+    def whole(t, way):
+        return (0, 4) if t < 4 else ((0, 2), (2, 4))[way]
+
+    def b_copy(t, way, ck):
         return pltpu.make_async_remote_copy(
-            bsend.at[cls * 4 + i], brecv.at[slot], b_s.at[cls, a], b_r.at[slot],
-            device_id=along(1 - cls, dist), device_id_type=MESH,
+            bsend.at[t - 1, way, ck], brecv.at[t - 1, way, ck],
+            b_s.at[t - 1, way, ck], b_r.at[t - 1, way, ck],
+            device_id=next_to(t % 2 == 0, way), device_id_type=MESH,
         )
+
+    def b_total(t, way, ck, o):
+        num = acc[o, pl.ds(ck * 2, 2)].reshape(256, 128)
+        dd = den[o]
+        if t < 4:
+            wide = brecv[t, way, ck].astype(F32)
+            num = num + wide[0:256]
+            dd = dd + wide[256:264] + wide[264:272]
+        return num, dd
+
+    def b_hop(t, way):
+        o = tile_at(t % 2 == 0, t * (1 - 2 * way))
+
+        def send(ck, carry, further):
+            if further:
+                b_copy(t + 1, way, ck).wait_recv()
+            num, dd = b_total(t if further else 4, way, ck, o)
+            high = dd.astype(BF)
+            low = (dd - high.astype(F32)).astype(BF)
+            bsend[t - 1, way, ck, pl.ds(0, 256), :] = num.astype(BF)
+            bsend[t - 1, way, ck, pl.ds(256, 16), :] = jnp.concatenate([high, low], axis=0)
+            b_copy(t, way, ck).start()
+            return carry
+
+        lo, hi = whole(t, way)
+        flo, fhi = whole(t + 1, way) if t < 4 else (0, 0)
+        if lo < flo:
+            lax.fori_loop(lo, flo, functools.partial(send, further=False), 0)
+        if max(lo, fhi) < hi:
+            lax.fori_loop(max(lo, fhi), hi, functools.partial(send, further=False), 0)
+        if flo < fhi:
+            lax.fori_loop(flo, fhi, functools.partial(send, further=True), 0)
 
     for cls in range(2):
         arrive(3, cls)
 
-    def last(t, carry):
-        cls, a = lax.rem(t, 2), t // 2
-        dist, i = b_parts(cls, a)
-        tile_step(3, cls, i)
-        o = cls * 4 + i
-
-        @pl.when(dist > 0)
-        def _():
-            for m in range(8):
-                bsend[o, pl.ds(m * 128, 128), :] = acc[o, :, pl.ds(m * 128, 128)].astype(BF)
-            dd = den[o]
-            high = dd.astype(BF)
-            low = (dd - high.astype(F32)).astype(BF)
-            bsend[o, pl.ds(1024, 16), :] = jnp.concatenate([high, low], axis=0)
-            b_copy(cls, a).start()
-
-        return carry
-
-    lax.fori_loop(0, 8, last, 0)
-
-    own = q * 4 + ((1 - q) * z + q * y) // 2
-    dsum = den[own]
-    for d in range(7):
+    def last(o):
+        tile_step(3, o // 4, lax.rem(o, 4))
+
+    last(tile_at(True, 4))
+    for way in range(2):
+        b_hop(4, way)
+    for t in (3, 2, 1):
+        for way in range(2):
+            last(tile_at(t % 2 == 0, t * (1 - 2 * way)))
+        for way in range(2):
+            b_hop(t, way)
+    own = tile_at(True, 0)
+    last(own)
+
+    def c_copy(t, way, ck):
+        o = tile_at(t % 2 == 1, -(t - 1) * (1 - 2 * way))
+        rows = pl.ds(pl.multiple_of(ck * 256, 256), 256)
+        return pltpu.make_async_remote_copy(
+            flux.at[o, rows], flux.at[o, rows], c_s.at[t - 1, way, ck], c_r.at[o, ck],
+            device_id=next_to(t % 2 == 1, way), device_id_type=MESH,
+        )
+
+    def c_arrive(o, ck):
+        rows = pl.ds(pl.multiple_of(ck * 256, 256), 256)
         pltpu.make_async_remote_copy(
-            bsend.at[0], brecv.at[d], b_s.at[0, 0], b_r.at[d],
-            device_id=along(0, 1), device_id_type=MESH,
+            flux.at[o, rows], flux.at[o, rows], c_s.at[0, 0, 0], c_r.at[o, ck],
+            device_id=next_to(True, 0), device_id_type=MESH,
         ).wait_recv()
-        two = brecv[d, pl.ds(1024, 16), :].astype(F32)
-        dsum = dsum + two[0:8] + two[8:16]
-    dtot[...] = jnp.maximum(dsum, 1.0)
-
-    def finish(m, carry):
-        rows = pl.ds(pl.multiple_of(m * 128, 128), 128)
-        num = acc[own, :, rows]
-        for d in range(7):
-            num += brecv[d, rows, :].astype(F32)
-        g = (num / dtot[pl.ds(m, 1), :]).T.astype(BF)
-        grid_out[rows, :] = g
-        mixed = jnp.dot(g, coag[...], preferred_element_type=F32)
-        flux[own, rows, :] = (gain[...] * jnp.tanh(mixed)).astype(BF)
-        return carry
-
-    lax.fori_loop(0, 8, finish, 0)
-
-    def c_copy(dist):
-        return pltpu.make_async_remote_copy(
-            flux.at[own], flux.at[own], c_s.at[dist - 1], c_r.at[own],
-            device_id=along(1 - q, dist), device_id_type=MESH,
-        )
-
-    for dist in ORDER:
-        c_copy(dist).start()
+
+    def finish(ck, carry):
+        for way in range(2):
+            b_copy(1, way, ck).wait_recv()
+        wide = brecv[0, 0, ck].astype(F32) + brecv[0, 1, ck].astype(F32)
+        dtot[...] = jnp.maximum(den[own] + wide[256:264] + wide[264:272], 1.0)
+        for h in range(2):
+            num = acc[own, ck * 2 + h] + wide[h * 128 : h * 128 + 128]
+            rows = pl.ds(pl.multiple_of(ck * 256 + h * 128, 128), 128)
+            g = (num / dtot[pl.ds(ck * 2 + h, 1), :]).T.astype(BF)
+            grid_out[rows, :] = g
+            mixed = jnp.dot(g, coag[...], preferred_element_type=F32)
+            flux[own, rows, :] = (gain[...] * jnp.tanh(mixed)).astype(BF)
+        for way in range(2):
+            c_copy(1, way, ck).start()
+        return carry
+
+    lax.fori_loop(0, 4, finish, 0)
 
     def d_copy(cls, i, dist):
         pair = pl.ds(i * 2, 2)
@@ -306,17 +339,8 @@
             device_id=along(cls, SIDE - dist), device_id_type=MESH,
         )
 
-    def back(t, carry):
-        o = lax.rem(own + t, 8)
+    def back(o):
         cls, i = o // 4, lax.rem(o, 4)
-
-        @pl.when(t > 0)
-        def _():
-            pltpu.make_async_remote_copy(
-                flux.at[o], flux.at[o], c_s.at[0], c_r.at[o],
-                device_id=along(0, 1), device_id_type=MESH,
-            ).wait_recv()
-
         tile = flux[o]
         for pos in range(4):
             r = jnp.dot(
@@ -331,9 +355,29 @@
                     dsend[cls, d - 1, pl.ds(i * 2, 2)] = two
         for dist in ORDER:
             d_copy(cls, i, dist).start()
-        return carry
-
-    lax.fori_loop(0, 8, back, 0)
+
+    back(own)
+    for t in (1, 2, 3):
+        tiles = [tile_at(t % 2 == 0, -t * (1 - 2 * way)) for way in range(2)]
+
+        def relay(ck, carry, t=t, tiles=tiles):
+            for way in range(2):
+                c_arrive(tiles[way], ck)
+                lo, hi = whole(t + 1, way)
+
+                @pl.when((ck >= lo) & (ck < hi))
+                def _():
+                    c_copy(t + 1, way, ck).start()
+
+            return carry
+
+        lax.fori_loop(0, 4, relay, 0)
+        for way in range(2):
+            back(tiles[way])
+    far = tile_at(True, 4)
+    for ck in range(4):
+        c_arrive(far, ck)
+    back(far)
 
     def gather_back(o, carry):
         for dist in range(1, SIDE):
@@ -351,7 +395,6 @@
     for dist in range(1, SIDE):
         for cls in range(2):
             a_copy(cls, dist).wait_send()
-        c_copy(dist).wait_send()
 
     @pl.when(strip < strips - 1)
     def _():
@@ -361,16 +404,11 @@
     def _():
         h_copy(1).wait_send()
 
-    def b_sent(t, carry):
-        cls, a = lax.rem(t, 2), t // 2
-
-        @pl.when(b_parts(cls, a)[0] > 0)
-        def _():
-            b_copy(cls, a).wait_send()
-
-        return carry
-
-    lax.fori_loop(0, 8, b_sent, 0)
+    for t in range(1, 5):
+        for way in range(2):
+            for ck in range(*whole(t, way)):
+                b_copy(t, way, ck).wait_send()
+                c_copy(t, way, ck).wait_send()
 
     def d_sent(o, carry):
         for dist in range(1, SIDE):
@@ -419,10 +457,10 @@
             pltpu.VMEM((2, 8, 8, 128), F32),
             pltpu.VMEM((2, 8, 8, 128), F32),
             pltpu.VMEM((8, 1024, 1024), BF),
-            pltpu.VMEM((8, 128, 1024), F32),
+            pltpu.VMEM((8, 8, 128, 128), F32),
             pltpu.VMEM((8, 8, 128), F32),
-            pltpu.VMEM((8, CHUNK, 128), BF),
-            pltpu.VMEM((7, CHUNK, 128), BF),
+            pltpu.VMEM((4, 2, 4, 272, 128), BF),
+            pltpu.VMEM((4, 2, 4, 272, 128), BF),
             pltpu.VMEM((8, 128), F32),
             pltpu.VMEM((8, 1024, 128), BF),
             pltpu.VMEM((2, 7, 8, 64, 128), BF),
@@ -432,8 +470,8 @@
             pltpu.VMEM((2, 128, 128), BF),
             pltpu.VMEM((2, 128, 128), BF),
             dma((2, 7)), dma((2, 7)),
-            dma((2, 4)), dma((7,)),
-            dma((7,)), dma((8,)),
+            dma((4, 2, 4)), dma((4, 2, 4)),
+            dma((4, 2, 4)), dma((8, 4)),
             dma((8, 7)), dma((8, 7)),
             dma((2,)), dma((2,)),
         ],

time: 172 us -> 136 us (0.79)
  the two profiles are of different devices: /device:TPU:1 before, /device:TPU:26 now
where the time goes in v2:
time: 136 us; the launch traced here: 135 us
  Pallas kernels  128 us (94%)
  local copies, waits for them, and re-layouts  5.42 us (4%)
  other arithmetic  1.62 us (1%)
    pallas_call x1, Pallas kernels, shards(): pl.pallas_call(kernel, out_shape=(jax.ShapeDtypeStruct((1024, chans), BF)...  128 us
    unnamed x8, local copies, waits for them, and re-layouts  4.99 us

profile of v2, /device:TPU:26, one launch (start us, length us, event | category | flops | bytes accessed | tf_op | source)
XLA Modules:
  0.0 135.4 jit_solution(3594568844938675040)
XLA Ops:
  0.6 0.0 copy-start.2
  0.7 0.6 copy-done.2
  1.3 0.2 convert_reduce_fusion
  1.5 0.0 copy-start
  1.5 0.6 select_reduce_fusion.1.tab
  2.1 0.0 copy-done
  2.1 0.0 copy-start.1
  2.1 0.1 iota_compare_fusion
  2.2 0.6 copy-done.1
  2.8 0.1 select_reduce_fusion
  2.9 0.1 copy.10
  3.0 0.2 broadcast_in_dim.53
  3.3 0.1 convert_element_type.13
  3.4 0.6 pad_maximum_fusion.tsel
  4.0 127.7 %shard_map.95 = (bf16[1024,128]{1,0:T(8,128)(2,1)}, bf16[48,64,128]{2,1,0:T(8,128)(2,1)}) custom-call(s32[128]{0:T(128)} %select_reduce_fusion.1.tab, s32[48]{0:T(128)} %copy-done, bf16[16,16,128]{2,1,0:T(8,128)(2,1)} %pad_maximum_fusion.tsel, bf16[48,64,128]{2,1,0:T(8,128)(2,1)} %bitcast.12, bf16[48,64,128]{2,1,0:T(8,128)(2,1)} %bitcast.13, ...), custom_call_target="tpu_custom_call" | custom-call | tf_op jit(solution)/shard_map/pallas_call | solution.py:446
  131.7 1.7 %copy.13 = bf16[1,1024,128]{2,1,0:T(8,128)(2,1)} copy(bf16[1,1024,128]{2,1,0:T(8,128)(2,1)} %bitcast.15) | data formatting | bytes 524288
  133.4 2.1 %copy.14 = bf16[1,3072,128]{2,1,0:T(8,128)(2,1)} copy(bf16[1,3072,128]{2,1,0:T(8,128)(2,1)} %bitcast.14) | data formatting | bytes 1572864
  (2 shorter events, 0.0 us)
Async XLA Ops:
  0.6 0.7 copy-start.2
  1.5 0.6 copy-start
  2.1 0.7 copy-start.1

commit v3 on v2

v3 whole, which is shorter than its diff:
```python
import jax
import jax.numpy as jnp
from jax import lax
from jax.experimental import pallas as pl
from jax.experimental.pallas import tpu as pltpu
from jax.sharding import PartitionSpec as P

MESH = pl.DeviceIdType.MESH
BF = jnp.bfloat16
F32 = jnp.float32
SIDE = 8
CHUNKS = 8
ORDER = (4, 3, 5, 2, 6, 1, 7)
PARTS = 4


def kernel(
    tab, slot_of, tsel, cols, wts, hsend_idx, hrecv_idx, coag, gain,
    grid_out, cols_out,
    abuf_s, abuf_r, trecv, tf, tr, xt, wexp, acc, den, bsend, brecv, dtot, flux, dsend, drecv,
    relaxed, hrows, hsend, hrecv,
    t_s, t_r, a_s, a_r, b_s, b_r, c_s, c_r, d_s, d_r, h_s, h_r,
):
    strip = lax.axis_index("strip")
    dom = lax.axis_index("dom")
    strips = lax.axis_size("strip")
    y = dom // SIDE
    z = lax.rem(dom, SIDE)
    q = lax.rem(y + z, 2)

    def along(cls, dist):
        ny = lax.rem(y + (1 - cls) * dist + SIDE, SIDE)
        nz = lax.rem(z + cls * dist + SIDE, SIDE)
        return (strip, ny * SIDE + nz)

    barrier = pltpu.get_barrier_semaphore()
    for cls in range(2):
        for dist in range(1, SIDE):
            pl.semaphore_signal(barrier, inc=1, device_id=along(cls, dist), device_id_type=MESH)

    @pl.when(strip > 0)
    def _():
        pl.semaphore_signal(barrier, inc=1, device_id=(strip - 1, dom), device_id_type=MESH)

    @pl.when(strip < strips - 1)
    def _():
        pl.semaphore_signal(barrier, inc=1, device_id=(strip + 1, dom), device_id_type=MESH)

    def pack(dst, cls, dist):
        base = cls * 64 + dist * 8

        def one(k, carry):
            for r in range(2):
                j = tab[base + k * 2 + r]
                dst[k, pl.ds(r * 64, 64), :] = cols[j]
                dst[k, pl.ds(128 + r * 64, 64), :] = wts[j]
            return carry

        lax.fori_loop(0, PARTS, one, 0)

    def pack_far(t, carry):
        cls, dist = t // 7, lax.rem(t, 7) + 1
        pack(abuf_s.at[cls, dist - 1], cls, dist)
        return carry

    lax.fori_loop(0, 14, pack_far, 0)

    neighbours = (strip > 0).astype(jnp.int32) + (strip < strips - 1).astype(jnp.int32)
    pl.semaphore_wait(barrier, 14 + neighbours)

    def t_copy(cls, dist):
        return pltpu.make_async_remote_copy(
            tsel.at[cls * 8 + dist], trecv.at[cls, dist],
            t_s.at[cls, dist - 1], t_r.at[cls, dist - 1],
            device_id=along(cls, dist), device_id_type=MESH,
        )

    def a_copy(cls, dist, k):
        return pltpu.make_async_remote_copy(
            abuf_s.at[cls, dist - 1, k], abuf_r.at[cls, dist, k],
            a_s.at[cls, dist - 1, k], a_r.at[cls, dist - 1, k],
            device_id=along(cls, dist), device_id_type=MESH,
        )

    for dist in ORDER:
        for cls in range(2):
            t_copy(cls, dist).start()

    def a_start(k, carry):
        for dist in ORDER:
            for cls in range(2):
                a_copy(cls, dist, k).start()
        return carry

    lax.fori_loop(0, 2, a_start, 0)

    for cls in range(2):
        pack(abuf_r.at[cls, 0], cls, 0)
        trecv[cls, 0] = tsel[cls * 8]

    idx = jnp.concatenate(
        [hsend_idx[...], hrecv_idx[...], jnp.zeros((4, 128), jnp.int32)], axis=0
    ).astype(F32)
    idx_t = idx.T
    hrows[...] = jnp.zeros_like(hrows)

    def gather(kc, carry):
        block = cols[pl.ds(kc * 4, 4)].reshape(256, 128)
        lane = lax.broadcasted_iota(jnp.int32, (128, 256), 1) + kc * 256
        lane = lane.astype(F32)
        for l in range(4):
            hot = jnp.where(idx_t[:, l : l + 1] == lane, 1.0, 0.0).astype(BF)
            hrows[l] += jnp.dot(hot, block, preferred_element_type=F32)
        return carry

    lax.fori_loop(0, 12, gather, 0)
    hsend[...] = hrows[pl.ds(0, 2)].astype(BF)

    def h_copy(way):
        step = 1 - 2 * way
        return pltpu.make_async_remote_copy(
            hsend.at[way], hrecv.at[way], h_s.at[way], h_r.at[way],
            device_id=(strip + step, dom), device_id_type=MESH,
        )

    @pl.when(strip < strips - 1)
    def _():
        h_copy(0).start()

    @pl.when(strip > 0)
    def _():
        h_copy(1).start()

    par = jnp.where(lax.broadcasted_iota(jnp.int32, (1, 128), 1) >= 64, 1.0, 0.0)
    twice = 2.0 * lax.broadcasted_iota(jnp.int32, (8, 128), 0).astype(F32)
    den[...] = jnp.zeros_like(den)

    def expand(cls, o, d, k):
        for rr in range(2):
            w = abuf_r[cls, d, k, pl.ds(128 + rr * 64, 64), :]
            u = tf[cls, d, pl.ds(2 * k + rr, 1), :] - par
            v = tr[cls, d, pl.ds(2 * k + rr, 1), :] - par
            wf = w.astype(F32)
            wrf = pltpu.roll(wf, 64, 1)
            wr = wrf.astype(BF)
            total = jnp.sum(wf, axis=0, keepdims=True)
            turned = jnp.sum(wrf, axis=0, keepdims=True)
            den[o] += jnp.where(u == twice, total, 0.0) + jnp.where(v == twice, turned, 0.0)
            ub = jnp.broadcast_to(u, (16, 128))
            vb = jnp.broadcast_to(v, (16, 128))
            rows = pl.ds(pl.multiple_of(d * 128 + rr * 64, 64), 64)
            for m in range(8):
                a = jnp.where(ub == 2.0 * m, 1.0, 0.0).astype(BF)
                b = jnp.where(vb == 2.0 * m, 1.0, 0.0).astype(BF)
                a4 = jnp.concatenate([a] * 4, axis=0)
                b4 = jnp.concatenate([b] * 4, axis=0)
                wexp[o, rows, pl.ds(m * 128, 128)] = w * a4 + wr * b4

    hcoord = (1 - q) * z + q * y
    ccoord = (1 - q) * y + q * z

    def tile_at(home, t):
        coord = hcoord if home else ccoord
        return (q if home else 1 - q) * 4 + lax.rem(coord + t + SIDE, SIDE) // 2

    def next_to(home, way):
        return along(1 - q if home else q, 1 - 2 * way)

    def add_up(t):
        home = t % 2 == 0
        k = 3 - t if t < 4 else t - 4
        cls = q if home else 1 - q
        o = tile_at(home, t)

        def source(e, carry):
            far = jnp.where(lax.rem(e, 2) == 0, 4 - e // 2, 4 + e // 2)
            d = jnp.where(e == 0, 0, far)

            @pl.when(e > 0)
            def _():
                a_copy(cls, jnp.maximum(d, 1), k).wait_recv()

            expand(cls, o, d, k)
            lanes = pl.ds(pl.multiple_of(d * 128, 128), 128)
            xt[:, lanes] = abuf_r[cls, d, k, pl.ds(0, 128), :].T
            return carry

        lax.fori_loop(0, 8, source, 0)
        for mm in range(4):
            part = jnp.dot(xt[...], wexp[o, :, pl.ds(mm * 256, 256)], preferred_element_type=F32)
            for h in range(2):
                acc[o, 2 * mm + h] = part[:, h * 128 : h * 128 + 128]

    def see(e, carry):
        cls, d = e // 8, lax.rem(e, 8)

        @pl.when(d > 0)
        def _():
            t_copy(cls, jnp.maximum(d, 1)).wait_recv()

        t = trecv[cls, d].astype(F32)[0:8]
        tf[cls, d] = t
        tr[cls, d] = pltpu.roll(t, 64, 1)
        return carry

    lax.fori_loop(0, 16, see, 0)

    def whole(t, way):
        half = CHUNKS // 2
        return (0, CHUNKS) if t < 4 else ((0, half), (half, CHUNKS))[way]

    def b_copy(t, way, ck):
        return pltpu.make_async_remote_copy(
            bsend.at[t - 1, way, ck], brecv.at[t - 1, way, ck],
            b_s.at[t - 1, way, ck], b_r.at[t - 1, way, ck],
            device_id=next_to(t % 2 == 0, way), device_id_type=MESH,
        )

    def b_total(t, way, ck, o):
        num = acc[o, ck]
        dd = den[o]
        if t < 4:
            wide = brecv[t, way, ck].astype(F32)
            num = num + wide[0:128]
            dd = dd + wide[128:136] + wide[136:144]
        return num, dd

    def b_hop(t, ways):
        def send(ck, way):
            o = tile_at(t % 2 == 0, t * (1 - 2 * way))
            if t == 4:
                ship(t, way, ck, *b_total(4, way, ck, o))
            elif t == 3:
                lo, hi = whole(4, way)
                further = (ck >= lo) & (ck < hi)

                @pl.when(further)
                def _():
                    b_copy(4, way, ck).wait_recv()
                    ship(t, way, ck, *b_total(t, way, ck, o))

                @pl.when(jnp.logical_not(further))
                def _():
                    ship(t, way, ck, *b_total(4, way, ck, o))
            else:
                b_copy(t + 1, way, ck).wait_recv()
                ship(t, way, ck, *b_total(t, way, ck, o))

        def both(ck, carry):
            for way in ways:
                send(ck, way)
            return carry

        if t == 4:
            half = CHUNKS // 2

            def four(ck, carry):
                send(ck, 0)
                send(ck + half, 1)
                return carry

            lax.fori_loop(0, half, four, 0)
        else:
            lax.fori_loop(0, CHUNKS, both, 0)

    def ship(t, way, ck, num, dd):
        high = dd.astype(BF)
        low = (dd - high.astype(F32)).astype(BF)
        bsend[t - 1, way, ck, pl.ds(0, 128), :] = num.astype(BF)
        bsend[t - 1, way, ck, pl.ds(128, 16), :] = jnp.concatenate([high, low], axis=0)
        b_copy(t, way, ck).start()

    add_up(4)
    b_hop(4, (0, 1))
    a_start(2, 0)
    add_up(3)
    add_up(5)
    b_hop(3, (0, 1))
    a_start(3, 0)

    @pl.when(strip > 0)
    def _():
        h_copy(0).wait_recv()

    @pl.when(strip == 0)
    def _():
        hrecv[0] = jnp.zeros((128, 128), BF)

    @pl.when(strip < strips - 1)
    def _():
        h_copy(1).wait_recv()

    @pl.when(strip == strips - 1)
    def _():
        hrecv[1] = jnp.zeros((128, 128), BF)

    keep = (
        jnp.where(strip > 0, 0.5, 0.0).astype(F32),
        jnp.where(strip < strips - 1, 0.5, 0.0).astype(F32),
    )
    for way in range(2):
        delta = keep[way] * (hrecv[way].astype(F32) - hrows[2 + way])
        high = delta.astype(BF)
        hrows[2 + way] = delta
        hsplit = (high, (delta - high.astype(F32)).astype(BF))
        if way == 0:
            split0 = hsplit
        else:
            split1 = hsplit
    highs = jnp.concatenate([split0[0], split1[0]], axis=0)
    lows = jnp.concatenate([split0[1], split1[1]], axis=0)

    def relax(kc, carry):
        row = (lax.broadcasted_iota(jnp.int32, (256, 128), 0) + kc * 256)
        hot = jnp.concatenate(
            [
                jnp.where(row == hrecv_idx[pl.ds(0, 1), :], 1.0, 0.0).astype(BF),
                jnp.where(row == hrecv_idx[pl.ds(1, 1), :], 1.0, 0.0).astype(BF),
            ],
            axis=1,
        )
        moved = jnp.dot(hot, highs, preferred_element_type=F32)
        moved += jnp.dot(hot, lows, preferred_element_type=F32)
        block = cols[pl.ds(kc * 4, 4)].reshape(256, 128).astype(F32)
        relaxed[pl.ds(kc * 4, 4)] = (block + moved).reshape(4, 64, 128)
        return carry

    lax.fori_loop(0, 12, relax, 0)

    add_up(2)
    add_up(6)
    b_hop(2, (0, 1))
    add_up(1)
    add_up(7)
    b_hop(1, (0, 1))
    own = tile_at(True, 0)
    add_up(0)

    def c_copy(t, way, ck):
        o = tile_at(t % 2 == 1, -(t - 1) * (1 - 2 * way))
        rows = pl.ds(pl.multiple_of(ck * 128, 128), 128)
        return pltpu.make_async_remote_copy(
            flux.at[o, rows], flux.at[o, rows], c_s.at[t - 1, way, ck], c_r.at[o, ck],
            device_id=next_to(t % 2 == 1, way), device_id_type=MESH,
        )

    def c_arrive(o, ck):
        rows = pl.ds(pl.multiple_of(ck * 128, 128), 128)
        pltpu.make_async_remote_copy(
            flux.at[o, rows], flux.at[o, rows], c_s.at[0, 0, 0], c_r.at[o, ck],
            device_id=next_to(True, 0), device_id_type=MESH,
        ).wait_recv()

    def finish(ck, carry):
        for way in range(2):
            b_copy(1, way, ck).wait_recv()
        wide = brecv[0, 0, ck].astype(F32) + brecv[0, 1, ck].astype(F32)
        dtot[...] = jnp.maximum(den[own] + wide[128:136] + wide[136:144], 1.0)
        rows = pl.ds(pl.multiple_of(ck * 128, 128), 128)
        g = ((acc[own, ck] + wide[0:128]) / dtot[pl.ds(ck, 1), :]).T.astype(BF)
        grid_out[rows, :] = g
        mixed = jnp.dot(g, coag[...], preferred_element_type=F32)
        flux[own, rows, :] = (gain[...] * jnp.tanh(mixed)).astype(BF)
        for way in range(2):
            c_copy(1, way, ck).start()
        return carry

    lax.fori_loop(0, CHUNKS, finish, 0)

    def d_copy(cls, k, dist):
        pair = pl.ds(k * 2, 2)
        o = cls * 4 + k
        return pltpu.make_async_remote_copy(
            dsend.at[cls, dist - 1, pair], drecv.at[pl.ds(cls * 64 + dist * 8 + k * 2, 2)],
            d_s.at[o, dist - 1], d_r.at[o, dist - 1],
            device_id=along(cls, SIDE - dist), device_id_type=MESH,
        )

    def back(o, k):
        cls = o // 4
        tile = flux[o]
        for pos in range(4):
            r = jnp.dot(
                wexp[o, pl.ds(pos * 256, 256), :], tile, preferred_element_type=F32
            ).astype(BF)
            for h in range(2):
                d = pos * 2 + h
                two = r[h * 128 : h * 128 + 128].reshape(2, 64, 128)
                if d == 0:
                    drecv[pl.ds(cls * 64 + k * 2, 2)] = two
                else:
                    dsend[cls, d - 1, pl.ds(k * 2, 2)] = two
        for dist in ORDER:
            d_copy(cls, k, dist).start()

    waiting = [(own, 3)]
    for t in (1, 2, 3):
        tiles = [tile_at(t % 2 == 0, -t * (1 - 2 * way)) for way in range(2)]

        def relay(ck, carry, t=t, tiles=tiles):
            for way in range(2):
                c_arrive(tiles[way], ck)
                lo, hi = whole(t + 1, way)

                @pl.when((ck >= lo) & (ck < hi))
                def _():
                    c_copy(t + 1, way, ck).start()

            return carry

        lax.fori_loop(0, CHUNKS, relay, 0)
        for pair in waiting:
            back(*pair)
        waiting = [(tiles[way], 4 - t - way) for way in range(2)]
    for pair in waiting:
        back(*pair)
    far = tile_at(True, 4)
    for ck in range(CHUNKS):
        c_arrive(far, ck)
    back(far, 0)

    def gather_back(o, carry):
        for dist in range(1, SIDE):
            d_copy(o // 4, lax.rem(o, 4), dist).wait_recv()
        return carry

    lax.fori_loop(0, 8, gather_back, 0)

    def final(j, carry):
        cols_out[j] = (relaxed[j] + drecv[slot_of[j]].astype(F32)).astype(BF)
        return carry

    lax.fori_loop(0, 48, final, 0)

    def a_sent(k, carry):
        for dist in range(1, SIDE):
            for cls in range(2):
                a_copy(cls, dist, k).wait_send()
        return carry

    lax.fori_loop(0, PARTS, a_sent, 0)
    for dist in range(1, SIDE):
        for cls in range(2):
            t_copy(cls, dist).wait_send()

    @pl.when(strip < strips - 1)
    def _():
        h_copy(0).wait_send()

    @pl.when(strip > 0)
    def _():
        h_copy(1).wait_send()

    for t in range(1, 5):
        for way in range(2):
            for ck in range(*whole(t, way)):
                b_copy(t, way, ck).wait_send()
                c_copy(t, way, ck).wait_send()

    def d_sent(o, carry):
        for dist in range(1, SIDE):
            d_copy(o // 4, lax.rem(o, 4), dist).wait_send()
        return carry

    lax.fori_loop(0, 8, d_sent, 0)


def shards(
    columns, regrid_weights, owner_table, grid_targets, halo_send, halo_recv, coag, settle_gain
):
    nblocks, blk, chans = regrid_weights.shape[1], regrid_weights.shape[2], columns.shape[2]
    dom = lax.axis_index("dom")
    y, z = dom // SIDE, lax.rem(dom, SIDE)
    owners = owner_table[0, :, 0]
    ids = jnp.arange(nblocks, dtype=jnp.int32)
    rank = jnp.sum(
        ((owners[:, None] == owners[None, :]) & (ids[None, :] < ids[:, None])).astype(jnp.int32),
        axis=1,
    )
    oy, oz = owners // SIDE, lax.rem(owners, SIDE)
    cls = lax.rem(oy + oz, 2)
    dist = jnp.where(cls == 0, oy - y + SIDE, oz - z + SIDE) % SIDE
    away = jnp.where(cls == 0, oz - z + SIDE, oy - y + SIDE) % SIDE
    slot_of = cls * 64 + dist * 8 + jnp.where(away < 4, 3 - away, away - 4) * 2 + rank
    hot = slot_of[None, :] == jnp.arange(128, dtype=jnp.int32)[:, None]
    tab = jnp.max(jnp.where(hot, ids[None, :], 0), axis=1)
    t01 = jnp.max(jnp.where(hot[:, None, :], grid_targets[0].T[None], -1), axis=2)
    tsel = jnp.repeat(t01, 64, axis=1).astype(BF).reshape(16, 8, 128)
    tsel = jnp.concatenate([tsel, tsel], axis=1)

    vmem = pl.BlockSpec(memory_space=pltpu.VMEM)
    smem = pl.BlockSpec(memory_space=pltpu.SMEM)
    dma = pltpu.SemaphoreType.DMA
    grid, out = pl.pallas_call(
        kernel,
        out_shape=(
            jax.ShapeDtypeStruct((1024, chans), BF),
            jax.ShapeDtypeStruct((nblocks, blk, chans), BF),
        ),
        in_specs=[smem, smem] + [vmem] * 7,
        out_specs=(vmem, vmem),
        scratch_shapes=[
            pltpu.VMEM((2, 7, PARTS, 256, 128), BF),
            pltpu.VMEM((2, 8, PARTS, 256, 128), BF),
            pltpu.VMEM((2, 8, 16, 128), BF),
            pltpu.VMEM((2, 8, 8, 128), F32),
            pltpu.VMEM((2, 8, 8, 128), F32),
            pltpu.VMEM((128, 1024), BF),
            pltpu.VMEM((8, 1024, 1024), BF),
            pltpu.VMEM((8, 8, 128, 128), F32),
            pltpu.VMEM((8, 8, 128), F32),
            pltpu.VMEM((4, 2, CHUNKS, 144, 128), BF),
            pltpu.VMEM((4, 2, CHUNKS, 144, 128), BF),
            pltpu.VMEM((8, 128), F32),
            pltpu.VMEM((8, 1024, 128), BF),
            pltpu.VMEM((2, 7, 8, 64, 128), BF),
            pltpu.VMEM((128, 64, 128), BF),
            pltpu.VMEM((48, 64, 128), F32),
            pltpu.VMEM((4, 128, 128), F32),
            pltpu.VMEM((2, 128, 128), BF),
            pltpu.VMEM((2, 128, 128), BF),
            dma((2, 7)), dma((2, 7)),
            dma((2, 7, PARTS)), dma((2, 7, PARTS)),
            dma((4, 2, CHUNKS)), dma((4, 2, CHUNKS)),
            dma((4, 2, CHUNKS)), dma((8, CHUNKS)),
            dma((8, 7)), dma((8, 7)),
            dma((2,)), dma((2,)),
        ],
        compiler_params=pltpu.CompilerParams(
            collective_id=0, has_side_effects=True, vmem_limit_bytes=56 * 2**20
        ),
    )(
        tab, slot_of, tsel,
        columns[0].reshape(nblocks, blk, chans), regrid_weights[0],
        halo_send[0, 0], halo_recv[0, 0], coag, settle_gain[None, :],
    )
    return grid[None], out.reshape(1, nblocks * blk, chans)


def solution(mesh):
    placed = (
        P("strip", "dom", None),
        P("strip", "dom", None, None),
        P("strip", "dom", None),
        P("strip", "dom", None),
        P("strip", "dom", None, None),
        P("strip", "dom", None, None),
        P(),
        P(),
    )
    return jax.shard_map(
        shards,
        mesh=mesh,
        in_specs=placed,
        out_specs=(P("strip", "dom", None), P("strip", "dom", None)),
        check_vma=False,
    )
```

time: 136 us -> 128 us (0.941)
  the two profiles are of different devices: /device:TPU:26 before, /device:TPU:1 now
where the time goes in v3:
time: 128 us
  Pallas kernels  120 us (94%)
  local copies, waits for them, and re-layouts  5.42 us (4%)
  other arithmetic  1.62 us (1%)
    pallas_call x1, Pallas kernels, shards(): pl.pallas_call(kernel, out_shape=(jax.ShapeDtypeStruct((1024, chans), BF)...  120 us
    unnamed x8, local copies, waits for them, and re-layouts  4.99 us

profile of v3, /device:TPU:1, one launch (start us, length us, event | category | flops | bytes accessed | tf_op | source)
XLA Modules:
  0.0 127.7 jit_solution(1359559217896401259)
XLA Ops:
  0.6 0.0 copy-start.2
  0.7 0.6 copy-done.2
  1.3 0.2 convert_reduce_fusion
  1.5 0.0 copy-start
  1.5 0.6 select_reduce_fusion.1.tab
  2.1 0.0 copy-done
  2.1 0.0 copy-start.1
  2.1 0.1 iota_compare_fusion
  2.2 0.6 copy-done.1
  2.8 0.1 select_reduce_fusion
  2.9 0.1 copy.10
  3.0 0.2 broadcast_in_dim.53
  3.3 0.1 convert_element_type.13
  3.4 0.6 pad_maximum_fusion.tsel
  4.0 119.9 %shard_map.95 = (bf16[1024,128]{1,0:T(8,128)(2,1)}, bf16[48,64,128]{2,1,0:T(8,128)(2,1)}) custom-call(s32[128]{0:T(128)} %select_reduce_fusion.1.tab, s32[48]{0:T(128)} %copy-done, bf16[16,16,128]{2,1,0:T(8,128)(2,1)} %pad_maximum_fusion.tsel, bf16[48,64,128]{2,1,0:T(8,128)(2,1)} %bitcast.12, bf16[48,64,128]{2,1,0:T(8,128)(2,1)} %bitcast.13, ...), custom_call_target="tpu_custom_call" | custom-call | tf_op jit(solution)/shard_map/pallas_call | solution.py:494
  124.0 1.7 %copy.13 = bf16[1,1024,128]{2,1,0:T(8,128)(2,1)} copy(bf16[1,1024,128]{2,1,0:T(8,128)(2,1)} %bitcast.15) | data formatting | bytes 524288
  125.6 2.1 %copy.14 = bf16[1,3072,128]{2,1,0:T(8,128)(2,1)} copy(bf16[1,3072,128]{2,1,0:T(8,128)(2,1)} %bitcast.14) | data formatting | bytes 1572864
  (2 shorter events, 0.0 us)
Async XLA Ops:
  0.6 0.7 copy-start.2
  1.5 0.6 copy-start
  2.1 0.7 copy-start.1

commit v4 on v3

--- a/solution.py
+++ b/solution.py
@@ -419,19 +419,6 @@
         c_arrive(far, ck)
     back(far, 0)
 
-    def gather_back(o, carry):
-        for dist in range(1, SIDE):
-            d_copy(o // 4, lax.rem(o, 4), dist).wait_recv()
-        return carry
-
-    lax.fori_loop(0, 8, gather_back, 0)
-
-    def final(j, carry):
-        cols_out[j] = (relaxed[j] + drecv[slot_of[j]].astype(F32)).astype(BF)
-        return carry
-
-    lax.fori_loop(0, 48, final, 0)
-
     def a_sent(k, carry):
         for dist in range(1, SIDE):
             for cls in range(2):
@@ -456,6 +443,19 @@
             for ck in range(*whole(t, way)):
                 b_copy(t, way, ck).wait_send()
                 c_copy(t, way, ck).wait_send()
+
+    def gather_back(o, carry):
+        for dist in range(1, SIDE):
+            d_copy(o // 4, lax.rem(o, 4), dist).wait_recv()
+        return carry
+
+    lax.fori_loop(0, 8, gather_back, 0)
+
+    def final(j, carry):
+        cols_out[j] = (relaxed[j] + drecv[slot_of[j]].astype(F32)).astype(BF)
+        return carry
+
+    lax.fori_loop(0, 48, final, 0)
 
     def d_sent(o, carry):
         for dist in range(1, SIDE):

time: 128 us -> 128 us (level)
  no operation moved by 1% of the time
where the time goes in v4:
time: 128 us; the launch traced here: 127 us
  Pallas kernels  120 us (94%)
  local copies, waits for them, and re-layouts  5.42 us (4%)
  other arithmetic  1.62 us (1%)
    pallas_call x1, Pallas kernels, shards(): pl.pallas_call(kernel, out_shape=(jax.ShapeDtypeStruct((1024, chans), BF)...  120 us
    unnamed x8, local copies, waits for them, and re-layouts  4.99 us

profile of v4, /device:TPU:1, one launch (start us, length us, event | category | flops | bytes accessed | tf_op | source)
XLA Modules:
  0.0 127.4 jit_solution(11569873545832493869)
XLA Ops:
  0.6 0.0 copy-start.2
  0.7 0.6 copy-done.2
  1.3 0.2 convert_reduce_fusion
  1.5 0.0 copy-start
  1.5 0.6 select_reduce_fusion.1.tab
  2.1 0.0 copy-done
  2.1 0.0 copy-start.1
  2.1 0.1 iota_compare_fusion
  2.2 0.6 copy-done.1
  2.8 0.1 select_reduce_fusion
  2.9 0.1 copy.10
  3.0 0.2 broadcast_in_dim.53
  3.3 0.1 convert_element_type.13
  3.4 0.6 pad_maximum_fusion.tsel
  4.0 119.7 %shard_map.95 = (bf16[1024,128]{1,0:T(8,128)(2,1)}, bf16[48,64,128]{2,1,0:T(8,128)(2,1)}) custom-call(s32[128]{0:T(128)} %select_reduce_fusion.1.tab, s32[48]{0:T(128)} %copy-done, bf16[16,16,128]{2,1,0:T(8,128)(2,1)} %pad_maximum_fusion.tsel, bf16[48,64,128]{2,1,0:T(8,128)(2,1)} %bitcast.12, bf16[48,64,128]{2,1,0:T(8,128)(2,1)} %bitcast.13, ...), custom_call_target="tpu_custom_call" | custom-call | tf_op jit(solution)/shard_map/pallas_call | solution.py:494
  123.7 1.7 %copy.13 = bf16[1,1024,128]{2,1,0:T(8,128)(2,1)} copy(bf16[1,1024,128]{2,1,0:T(8,128)(2,1)} %bitcast.15) | data formatting | bytes 524288
  125.3 2.1 %copy.14 = bf16[1,3072,128]{2,1,0:T(8,128)(2,1)} copy(bf16[1,3072,128]{2,1,0:T(8,128)(2,1)} %bitcast.14) | data formatting | bytes 1572864
  (2 shorter events, 0.0 us)
Async XLA Ops:
  0.6 0.7 copy-start.2
  1.5 0.6 copy-start
  2.1 0.7 copy-start.1

commit v5 on v4

--- a/solution.py
+++ b/solution.py
@@ -409,9 +409,11 @@
             return carry
 
         lax.fori_loop(0, CHUNKS, relay, 0)
-        for pair in waiting:
-            back(*pair)
-        waiting = [(tiles[way], 4 - t - way) for way in range(2)]
+        if t != 2:
+            for pair in waiting:
+                back(*pair)
+            waiting = []
+        waiting = waiting + [(tiles[way], 4 - t - way) for way in range(2)]
     for pair in waiting:
         back(*pair)
     far = tile_at(True, 4)

time: 128 us -> 130 us (1.016)
  Pallas kernels: 120 us -> 122 us
    pallas_call x1, Pallas kernels: 120 us -> 122 us  [shards(): pl.pallas_call(kernel, out_shape=(jax.ShapeDtypeStruct((1024, chans), BF)...]
where the time goes in v5:
time: 130 us
  Pallas kernels  122 us (94%)
  local copies, waits for them, and re-layouts  5.42 us (4%)
  other arithmetic  1.62 us (1%)
    pallas_call x1, Pallas kernels, shards(): pl.pallas_call(kernel, out_shape=(jax.ShapeDtypeStruct((1024, chans), BF)...  122 us
    unnamed x8, local copies, waits for them, and re-layouts  4.99 us

profile of v5, /device:TPU:1, one launch (start us, length us, event | category | flops | bytes accessed | tf_op | source)
XLA Modules:
  0.0 129.8 jit_solution(5523214759587081055)
XLA Ops:
  0.6 0.0 copy-start.2
  0.7 0.6 copy-done.2
  1.3 0.2 convert_reduce_fusion
  1.5 0.0 copy-start
  1.5 0.6 select_reduce_fusion.1.tab
  2.1 0.0 copy-done
  2.1 0.0 copy-start.1
  2.1 0.1 iota_compare_fusion
  2.2 0.6 copy-done.1
  2.8 0.1 select_reduce_fusion
  2.9 0.1 copy.10
  3.0 0.2 broadcast_in_dim.53
  3.3 0.1 convert_element_type.13
  3.4 0.6 pad_maximum_fusion.tsel
  4.0 122.1 %shard_map.95 = (bf16[1024,128]{1,0:T(8,128)(2,1)}, bf16[48,64,128]{2,1,0:T(8,128)(2,1)}) custom-call(s32[128]{0:T(128)} %select_reduce_fusion.1.tab, s32[48]{0:T(128)} %copy-done, bf16[16,16,128]{2,1,0:T(8,128)(2,1)} %pad_maximum_fusion.tsel, bf16[48,64,128]{2,1,0:T(8,128)(2,1)} %bitcast.12, bf16[48,64,128]{2,1,0:T(8,128)(2,1)} %bitcast.13, ...), custom_call_target="tpu_custom_call" | custom-call | tf_op jit(solution)/shard_map/pallas_call | solution.py:496
  126.1 1.7 %copy.13 = bf16[1,1024,128]{2,1,0:T(8,128)(2,1)} copy(bf16[1,1024,128]{2,1,0:T(8,128)(2,1)} %bitcast.15) | data formatting | bytes 524288
  127.7 2.1 %copy.14 = bf16[1,3072,128]{2,1,0:T(8,128)(2,1)} copy(bf16[1,3072,128]{2,1,0:T(8,128)(2,1)} %bitcast.14) | data formatting | bytes 1572864
  (2 shorter events, 0.0 us)
Async XLA Ops:
  0.6 0.7 copy-start.2
  1.5 0.6 copy-start
  2.1 0.7 copy-start.1
